TPU v7x, 32 devices: a whole 2x2x4 slice. The times are simulated.
32 devices in a mesh: tm: 4 (over y, x), space: 8 (over z, core).
Axes of the slice: x: 2, y: 2, z: 4, core: 2. Of those that a mesh axis runs over, the one named last changes fastest.
Arguments:
- starts: float32 [4, 8, 32, 128, 128], P('tm', None, 'space'), may hold values from -6 to 6
- classes: int32 [32, 128, 128], P('space'), may hold values from 0 to 15
- dispersion_table: float32 [16, 8], replicated, may hold values from 0.0015 to 0.015
- mixing: float32 [8, 8], replicated, may hold values from -0.04 to 1, as said below
Outputs:
- slice_ends: float32 [4, 8, 32, 128, 128], P('tm', None, 'space')
Inputs may be any that keep to these rules, and one draw needn't show every extreme that they name: mixing has 1 minus a positive decay rate of at most 0.3 on its diagonal, and off-diagonal couplings between -0.04 and 0.04.
All inputs are finite; a program needn't handle non-finite values.
Results may differ from a plain program's by a relative error of at most 0.00013.
Values sent between devices are 32-bit elements; how exact they have to be, the bound alone decides.
A program may use at most 128 MiB of HBM per device.

v0:
```python
import jax
import jax.numpy as jnp
from jax import lax
from jax.sharding import PartitionSpec as P

corner_weights = (1.0, 0.5, 0.25)
fine_courant = (0.15, 0.1, 0.05)
coarse_courant = (0.3, 0.2, 0.1)


def with_halo(cells, sides, width):
    for axis, dim in sides:
        count = lax.axis_size(axis)
        ends = count - 1
        head = lax.slice_in_dim(cells, 0, width, axis=dim)
        tail = lax.slice_in_dim(cells, cells.shape[dim] - width, cells.shape[dim], axis=dim)
        cells = jnp.concatenate(
            [
                lax.ppermute(tail, axis, [(i, (i + 1) % count) for i in range(ends)]),
                cells,
                lax.ppermute(head, axis, [((i + 1) % count, i) for i in range(ends)]),
            ],
            axis=dim,
        )
    return cells


def from_behind(value, axis, by):
    size = lax.axis_size(axis)
    pairs = [(i, i + by) for i in range(size) if 0 <= i + by < size]
    return lax.ppermute(value, axis, pairs)


def advance(padded, kappa, coarse_form):
    extent_x = padded.shape[1] - 2
    extent_y = padded.shape[2] - 2
    extent_z = padded.shape[3] - 2
    centre = padded[:, 1 : 1 + extent_x, 1 : 1 + extent_y, 1 : 1 + extent_z]
    kappa_here = kappa[:, 1 : 1 + extent_x, 1 : 1 + extent_y, 1 : 1 + extent_z]
    summed = jnp.zeros_like(centre)
    for shift_x in (-1, 0, 1):
        for shift_y in (-1, 0, 1):
            for shift_z in (-1, 0, 1):
                order_level = abs(shift_x) + abs(shift_y) + abs(shift_z)
                if order_level == 0:
                    continue
                if coarse_form and order_level > 1:
                    continue
                weight = 2.0 if coarse_form else 0.5 * corner_weights[order_level - 1]
                neighbour = padded[
                    :,
                    1 + shift_x : 1 + shift_x + extent_x,
                    1 + shift_y : 1 + shift_y + extent_y,
                    1 + shift_z : 1 + shift_z + extent_z,
                ]
                kappa_near = kappa[
                    :,
                    1 + shift_x : 1 + shift_x + extent_x,
                    1 + shift_y : 1 + shift_y + extent_y,
                    1 + shift_z : 1 + shift_z + extent_z,
                ]
                summed = summed + weight * (kappa_here + kappa_near) * (neighbour - centre)
    courant = coarse_courant if coarse_form else fine_courant
    upwind = courant[0] * (centre - padded[:, 0:extent_x, 1 : 1 + extent_y, 1 : 1 + extent_z])
    upwind = upwind + courant[1] * (
        centre - padded[:, 1 : 1 + extent_x, 0:extent_y, 1 : 1 + extent_z]
    )
    upwind = upwind + courant[2] * (
        centre - padded[:, 1 : 1 + extent_x, 1 : 1 + extent_y, 0:extent_z]
    )
    return centre + summed - upwind


def species_mix(mixing, moved):
    return jnp.einsum("st,txyz->sxyz", mixing, moved, precision=lax.Precision.HIGHEST)


def pad_cross(field):
    return jnp.pad(field, ((0, 0), (0, 0), (1, 1), (1, 1)))


def body(starts, classes, dispersion_table, mixing):
    field_start = starts[0]
    count_classes = dispersion_table.shape[0]
    extended = with_halo(classes, (("space", 0),), 2)
    extended = jnp.pad(extended, ((0, 0), (1, 1), (1, 1)))
    onehot = (
        extended[None] == jnp.arange(count_classes, dtype=jnp.int32)[:, None, None, None]
    ).astype(jnp.float32)
    kappa_full = jnp.einsum(
        "cs,cxyz->sxyz", dispersion_table, onehot, precision=lax.Precision.HIGHEST
    )
    kappa_one = kappa_full[:, 1:-1]
    tm_position = lax.axis_index("tm")

    def coarse(field):
        padded = pad_cross(with_halo(field, (("space", 1),), 1))
        return species_mix(mixing, advance(padded, kappa_one, True))

    coarse_old = coarse(field_start)
    field = field_start
    for fine_repeat in range(2):
        padded = pad_cross(with_halo(field, (("space", 1),), 1))
        field = species_mix(mixing, advance(padded, kappa_one, False))
    correction = field - coarse_old
    current_end = coarse_old + correction
    for repeat in range(lax.axis_size("tm") - 1):
        incoming = from_behind(current_end, "tm", 1)
        incoming = jnp.where(tm_position == 0, field_start, incoming)
        current_end = coarse(incoming) + correction
    return current_end[None]


def solution(mesh):
    in_specs = (P("tm", None, "space", None, None), P("space", None, None), P(), P())
    out_specs = P("tm", None, "space", None, None)
    return jax.shard_map(body, mesh=mesh, in_specs=in_specs, out_specs=out_specs, check_vma=False)
```

profile of v0, /device:TPU:12, one launch (start us, length us, event | category | flops | bytes accessed | tf_op | source)
XLA Modules:
  0.0 429.9 jit_solution(18121318664448060226)
XLA Ops:
  13.9 5.5 %fusion.5 = f32[8,8,130,130]{3,0,2,1:T(8,128)S(1)} fusion(s32[8,130,130]{2,1,0:T(8,128)S(1)} %pad.21, f32[16,8]{0,1:T(8,128)S(1)} %copy-done.20), kind=kOutput, calls=%fused_computation.20 | convolution fusion | flops 209830400 | bytes 4867712 | tf_op jit(solution)/shard_map/cs,cxyz->sxyz/dot_general | solution.py:90
  19.5 6.6 %slice_add_fusion.25 = (f32[8,4,128,128]{3,0,2,1:T(8,128)S(1)}, f32[8,4,128,128]{3,0,2,1:T(8,128)}, f32[8,4,128,128]{3,0,2,1:T(8,128)}, f32[8,4,128,128]{3,0,2,1...) fusion(f32[8,8,130,130]{3,0,2,1:T(8,128)S(1)} %fusion.5), kind=kLoop, calls=%fused_computation.293 | loop fusion | flops 3145728 | bytes 27262976 | tf_op jit(solution)/shard_map/add | solution.py:62
  26.1 4.3 %select_maximum_fusion.8 = f32[8,6,130,130]{3,0,2,1:T(8,128)} fusion(f32[8,1,128,128]{3,0,2,1:T(8,128)S(1)} %collective-permute-done.3, f32[8,4,128,128]{3,0,2,1:T(8,128)S(1)} %bitcast.57, f32[8,1,128,128]{3,0,2,1:T(8,128)S(1)} %collective-permute-done.2), kind=kLoop, calls=%fused_computation.15 | loop fusion | flops 12168000 | bytes 6390528 | tf_op jit(solution)/shard_map/concatenate | solution.py:17
  30.4 61.0 %fusion.494 = f32[8,4,128,128]{3,0,2,1:T(8,128)} fusion(f32[8,4,128,128]{3,0,2,1:T(8,128)} %bitcast.58, f32[8,6,130,130]{3,0,2,1:T(8,128)} %select_maximum_fusion.8, f32[8,4,128,128]{3,0,2,1:T(8,128)} %get-tuple-element.6, f32[8,4,128,128]{3,0,2,1:T(8,128)} %get-tuple-element.7, f32[8,4,128,128]{3,0,2,1:T(8,128)} %get-tuple-element.8, ...), kind=kLoop, calls=%fused_computation.177.clone.clone.clone.clone.1 | loop fusion | flops 70778880 | bytes 112197632 | tf_op jit(solution)/shard_map/st,txyz->sxyz/dot_general | solution.py:75
  95.1 3.9 collective-permute-start.5
  101.0 12.4 %fusion.305 = f32[4,128,128,8]{2,3,1,0:T(8,128)} fusion(f32[8,4,128,128]{3,0,2,1:T(8,128)} %bitcast.59, f32[8,6,130,130]{3,0,2,1:T(8,128)} %select_maximum_fusion.8, f32[8,4,128,128]{3,0,2,1:T(8,128)S(1)} %copy-done.2, f32[8,4,128,128]{3,0,2,1:T(8,128)S(1)} %copy-done.4, f32[8,4,128,128]{3,0,2,1:T(8,128)S(1)} %copy-done.6, ...), kind=kOutput, calls=%fused_computation.352 | convolution fusion | flops 68681728 | bytes 26214656 | tf_op jit(solution)/shard_map/st,txyz->sxyz/dot_general | solution.py:75
  115.0 4.3 %select_maximum_fusion.6 = f32[8,6,130,130]{3,0,2,1:T(8,128)} fusion(f32[8,1,128,128]{3,0,2,1:T(8,128)S(1)} %collective-permute-done.5, f32[8,4,128,128]{3,0,2,1:T(8,128)S(1)} %fusion.360, f32[8,1,128,128]{3,0,2,1:T(8,128)S(1)} %collective-permute-done.4), kind=kLoop, calls=%fused_computation.13 | loop fusion | flops 12168000 | bytes 6390528 | tf_op jit(solution)/shard_map/concatenate | solution.py:17
  119.3 61.9 %fusion.364.clone.4 = f32[8,4,128,128]{3,0,2,1:T(8,128)} fusion(f32[8,4,128,128]{3,0,2,1:T(8,128)} %copy-done.15, f32[8,6,130,130]{3,0,2,1:T(8,128)} %select_maximum_fusion.6, f32[8,1,128,128]{3,0,2,1:T(8,128)} %copy-done.17, f32[8,1,128,128]{3,0,2,1:T(8,128)} %copy-done.18, f32[8,4,128,128]{3,0,2,1:T(8,128)} %get-tuple-element.6, ...), kind=kLoop, calls=%fused_computation.94.clone.clone.clone.clone.clone.clone.1 | loop fusion | flops 70778880 | bytes 112197632 | tf_op jit(solution)/shard_map/add | solution.py:106
  181.1 6.2 %bitcast_add_fusion.3 = (f32[8,4,128,128]{3,0,2,1:T(8,128)}, f32[8,4,128,128]{3,0,2,1:T(8,128)}) fusion(f32[4,128,128,8]{2,3,1,0:T(8,128)} %fusion.305, f32[8,8]{1,0:T(8,128)S(1)} %copy-done, f32[8,4,128,128]{3,0,2,1:T(8,128)} %fusion.364.clone.4), kind=kOutput, calls=%fused_computation.299 | convolution fusion | flops 51380224 | bytes 8388864 | tf_op jit(solution)/shard_map/st,txyz->sxyz/dot_general | solution.py:75
  190.8 47.5 %collective-permute-done.6 = f32[8,4,128,128]{3,0,2,1:T(8,128)} collective-permute-done((f32[8,4,128,128]{3,0,2,1:T(8,128)}, f32[8,4,128,128]{3,0,2,1:T(8,128)}, u32[]{:S(2)}, u32[]{:S(2)}) %collective-permute-start.6) | collective-permute-done | bytes 2097184 | tf_op jit(solution)/shard_map/ppermute | solution.py:31
  247.1 4.3 %collective-permute-done.8 = f32[8,1,128,128]{3,0,2,1:T(8,128)S(1)} collective-permute-done((f32[8,1,128,128]{3,0,2,1:T(8,128)S(1)}, f32[8,1,128,128]{3,0,2,1:T(8,128)S(1)}, u32[]{:S(2)}, u32[]{:S(2)}) %collective-permute-start.8) | collective-permute-done | bytes 524320 | tf_op jit(solution)/shard_map/ppermute | solution.py:21
  251.4 4.1 collective-permute-done.7
  255.6 4.5 %select_maximum_fusion.4 = f32[8,6,130,130]{3,0,2,1:T(8,128)} fusion(f32[8,1,128,128]{3,0,2,1:T(8,128)S(1)} %collective-permute-done.8, f32[8,4,128,128]{3,0,2,1:T(8,128)S(1)} %broadcast_select_fusion.2, f32[8,1,128,128]{3,0,2,1:T(8,128)S(1)} %collective-permute-done.7), kind=kLoop, calls=%fused_computation.11 | loop fusion | flops 12168000 | bytes 6390528 | tf_op jit(solution)/shard_map/concatenate | solution.py:17
  260.2 10.8 %bitcast_add_fusion.2 = f32[8,4,128,128]{3,0,2,1:T(8,128)} fusion(f32[8,4,128,128]{3,0,2,1:T(8,128)S(1)} %copy-done.11, f32[8,4,128,128]{3,0,2,1:T(8,128)} %copy-done.13, f32[8,1,128,128]{3,0,2,1:T(8,128)S(1)} %collective-permute-done.8, f32[8,6,130,130]{3,0,2,1:T(8,128)} %select_maximum_fusion.4, f32[8,1,128,128]{3,0,2,1:T(8,128)S(1)} %collective-permute-done.7, ...), kind=kOutput, calls=%fused_computation.297 | convolution fusion | flops 69206016 | bytes 28311808 | tf_op jit(solution)/shard_map/st,txyz->sxyz/dot_general | solution.py:75
  273.5 47.3 %collective-permute-done.9 = f32[8,4,128,128]{3,0,2,1:T(8,128)S(1)} collective-permute-done((f32[8,4,128,128]{3,0,2,1:T(8,128)}, f32[8,4,128,128]{3,0,2,1:T(8,128)S(1)}, u32[]{:S(2)}, u32[]{:S(2)}) %collective-permute-start.9) | collective-permute-done | bytes 2097184 | tf_op jit(solution)/shard_map/ppermute | solution.py:31
  326.6 4.3 collective-permute-done.11
  330.8 3.8 collective-permute-done.10
  334.6 4.3 %select_maximum_fusion.2 = f32[8,6,130,130]{3,0,2,1:T(8,128)} fusion(f32[8,1,128,128]{3,0,2,1:T(8,128)S(1)} %collective-permute-done.11, f32[8,4,128,128]{3,0,2,1:T(8,128)S(1)} %broadcast_select_fusion.1, f32[8,1,128,128]{3,0,2,1:T(8,128)S(1)} %collective-permute-done.10), kind=kLoop, calls=%fused_computation.9 | loop fusion | flops 12168000 | bytes 6390528 | tf_op jit(solution)/shard_map/concatenate | solution.py:17
  339.0 10.8 %bitcast_add_fusion.1 = f32[8,4,128,128]{3,0,2,1:T(8,128)} fusion(f32[8,4,128,128]{3,0,2,1:T(8,128)S(1)} %copy-done.11, f32[8,4,128,128]{3,0,2,1:T(8,128)} %copy-done.14, f32[8,1,128,128]{3,0,2,1:T(8,128)S(1)} %collective-permute-done.11, f32[8,6,130,130]{3,0,2,1:T(8,128)} %select_maximum_fusion.2, f32[8,1,128,128]{3,0,2,1:T(8,128)S(1)} %collective-permute-done.10, ...), kind=kOutput, calls=%fused_computation.296 | convolution fusion | flops 69206016 | bytes 28311808 | tf_op jit(solution)/shard_map/st,txyz->sxyz/dot_general | solution.py:75
  351.7 47.8 %collective-permute-done.12 = f32[8,4,128,128]{3,0,2,1:T(8,128)S(1)} collective-permute-done((f32[8,4,128,128]{3,0,2,1:T(8,128)}, f32[8,4,128,128]{3,0,2,1:T(8,128)S(1)}, u32[]{:S(2)}, u32[]{:S(2)}) %collective-permute-start.12) | collective-permute-done | bytes 2097184 | tf_op jit(solution)/shard_map/ppermute | solution.py:31
  405.3 4.3 collective-permute-done.14
  409.5 3.8 collective-permute-done.13
  413.4 4.6 %select_maximum_fusion = f32[8,6,130,130]{3,0,2,1:T(8,128)} fusion(f32[8,1,128,128]{3,0,2,1:T(8,128)S(1)} %collective-permute-done.14, f32[8,4,128,128]{3,0,2,1:T(8,128)S(1)} %broadcast_select_fusion, f32[8,1,128,128]{3,0,2,1:T(8,128)S(1)} %collective-permute-done.13), kind=kLoop, calls=%fused_computation.7 | loop fusion | flops 12168000 | bytes 6390528 | tf_op jit(solution)/shard_map/concatenate | solution.py:17
  418.0 9.8 %fusion.253 = f32[1,8,4,128,128]{4,1,3,2,0:T(8,128)S(1)} fusion(f32[8,4,128,128]{3,0,2,1:T(8,128)S(1)} %copy-done.11, f32[8,4,128,128]{3,0,2,1:T(8,128)} %copy-done.12, f32[8,1,128,128]{3,0,2,1:T(8,128)S(1)} %collective-permute-done.14, f32[8,6,130,130]{3,0,2,1:T(8,128)} %select_maximum_fusion, f32[8,1,128,128]{3,0,2,1:T(8,128)S(1)} %collective-permute-done.13, ...), kind=kOutput, calls=%fused_computation.295 | convolution fusion | flops 69206016 | bytes 28311808 | tf_op jit(solution)/shard_map/st,txyz->sxyz/dot_general | solution.py:75
  (76 shorter events, 50.8 us)
Async XLA Ops:
  0.0 91.4 %copy-start = (f32[8,8]{1,0:T(8,128)S(1)}, f32[8,8]{1,0:T(8,128)}, u32[]{:S(2)}) copy-start(f32[8,8]{1,0:T(8,128)} %param.7) | copy-start | bytes 772
  1.0 12.5 %collective-permute-start.1 = (s32[2,128,128]{2,1,0:T(8,128)S(1)}, s32[2,128,128]{2,1,0:T(8,128)S(1)}, u32[]{:S(2)}, u32[]{:S(2)}) collective-permute-start(s32[2,128,128]{2,1,0:T(8,128)S(1)} %get-tuple-element.22), channel_id=1, source_target_pairs={{1,0},{2,1},{3,2},{4,3},{5,4},{6,5},{7,6},{9,8},{10,9},{11,10},{12... | collective-permute-start | bytes 393224 | tf_op jit(solution)/shard_map/ppermute | solution.py:21
  2.9 10.6 %collective-permute-start = (s32[2,128,128]{2,1,0:T(8,128)S(1)}, s32[2,128,128]{2,1,0:T(8,128)S(1)}, u32[]{:S(2)}, u32[]{:S(2)}) collective-permute-start(s32[2,128,128]{2,1,0:T(8,128)S(1)} %get-tuple-element.21), channel_id=1, source_target_pairs={{0,1},{1,2},{2,3},{3,4},{4,5},{5,6},{6,7},{8,9},{9,10},{10,11},{11... | collective-permute-start | bytes 393224 | tf_op jit(solution)/shard_map/ppermute | solution.py:19
  8.2 17.9 %copy-start.16 = (f32[1,8,4,128,128]{4,1,3,2,0:T(8,128)}, f32[1,8,4,128,128]{4,1,3,2,0:T(8,128)S(1)}, u32[]{:S(2)}) copy-start(f32[1,8,4,128,128]{4,1,3,2,0:T(8,128)S(1)} %copy.16) | copy-start | bytes 6291460
  8.3 17.8 %collective-permute-start.3 = (f32[8,1,128,128]{3,0,2,1:T(8,128)S(1)}, f32[8,1,128,128]{3,0,2,1:T(8,128)S(1)}, u32[]{:S(2)}, u32[]{:S(2)}) collective-permute-start(f32[8,1,128,128]{3,0,2,1:T(8,128)S(1)} %get-tuple-element.20), channel_id=1, source_target_pairs={{1,0},{2,1},{3,2},{4,3},{5,4},{6,5},{7,6},{9,8},{10,9},{11,10},{12... | collective-permute-start | bytes 1572872 | tf_op jit(solution)/shard_map/ppermute | solution.py:21
  11.6 14.5 %collective-permute-start.2 = (f32[8,1,128,128]{3,0,2,1:T(8,128)S(1)}, f32[8,1,128,128]{3,0,2,1:T(8,128)S(1)}, u32[]{:S(2)}, u32[]{:S(2)}) collective-permute-start(f32[8,1,128,128]{3,0,2,1:T(8,128)S(1)} %get-tuple-element.19), channel_id=1, source_target_pairs={{0,1},{1,2},{2,3},{3,4},{4,5},{5,6},{6,7},{8,9},{9,10},{10,11},{11... | collective-permute-start | bytes 1572872 | tf_op jit(solution)/shard_map/ppermute | solution.py:19
  95.0 18.4 %copy-start.15 = (f32[8,4,128,128]{3,0,2,1:T(8,128)}, f32[8,4,128,128]{3,0,2,1:T(8,128)S(1)}, u32[]{:S(2)}) copy-start(f32[8,4,128,128]{3,0,2,1:T(8,128)S(1)} %fusion.360) | copy-start | bytes 6291460
  95.1 18.2 %collective-permute-start.5 = (f32[8,1,128,128]{3,0,2,1:T(8,128)S(1)}, f32[8,1,128,128]{3,0,2,1:T(8,128)S(1)}, u32[]{:S(2)}, u32[]{:S(2)}) collective-permute-start(f32[8,1,128,128]{3,0,2,1:T(8,128)S(1)} %get-tuple-element.18), channel_id=1, source_target_pairs={{1,0},{2,1},{3,2},{4,3},{5,4},{6,5},{7,6},{9,8},{10,9},{11,10},{12... | collective-permute-start | bytes 1572872 | tf_op jit(solution)/shard_map/ppermute | solution.py:21
  99.0 14.3 %collective-permute-start.4 = (f32[8,1,128,128]{3,0,2,1:T(8,128)S(1)}, f32[8,1,128,128]{3,0,2,1:T(8,128)S(1)}, u32[]{:S(2)}, u32[]{:S(2)}) collective-permute-start(f32[8,1,128,128]{3,0,2,1:T(8,128)S(1)} %get-tuple-element.17), channel_id=1, source_target_pairs={{0,1},{1,2},{2,3},{3,4},{4,5},{5,6},{6,7},{8,9},{9,10},{10,11},{11... | collective-permute-start | bytes 1572872 | tf_op jit(solution)/shard_map/ppermute | solution.py:19
  187.4 50.9 %collective-permute-start.6 = (f32[8,4,128,128]{3,0,2,1:T(8,128)}, f32[8,4,128,128]{3,0,2,1:T(8,128)}, u32[]{:S(2)}, u32[]{:S(2)}) collective-permute-start(f32[8,4,128,128]{3,0,2,1:T(8,128)} %get-tuple-element.23), channel_id=1, source_target_pairs={{0,8},{8,16},{16,24},{1,9},{9,17},{17,25},{2,10},{10,18},{18,26},{... | collective-permute-start | bytes 6291464 | tf_op jit(solution)/shard_map/ppermute | solution.py:31
  238.3 21.8 %copy-start.11 = (f32[8,4,128,128]{3,0,2,1:T(8,128)S(1)}, f32[8,4,128,128]{3,0,2,1:T(8,128)}, u32[]{:S(2)}) copy-start(f32[8,4,128,128]{3,0,2,1:T(8,128)} %get-tuple-element.24) | copy-start | bytes 6291460
  242.0 18.2 %copy-start.13 = (f32[8,4,128,128]{3,0,2,1:T(8,128)}, f32[8,4,128,128]{3,0,2,1:T(8,128)S(1)}, u32[]{:S(2)}) copy-start(f32[8,4,128,128]{3,0,2,1:T(8,128)S(1)} %broadcast_select_fusion.2) | copy-start | bytes 6291460
  242.0 18.1 %copy-start.9 = (f32[8,4,128,128]{3,0,2,1:T(8,128)S(1)}, f32[8,4,128,128]{3,0,2,1:T(8,128)}, u32[]{:S(2)}) copy-start(f32[8,4,128,128]{3,0,2,1:T(8,128)} %get-tuple-element.10) | copy-start | bytes 6291460
  242.1 9.4 %collective-permute-start.8 = (f32[8,1,128,128]{3,0,2,1:T(8,128)S(1)}, f32[8,1,128,128]{3,0,2,1:T(8,128)S(1)}, u32[]{:S(2)}, u32[]{:S(2)}) collective-permute-start(f32[8,1,128,128]{3,0,2,1:T(8,128)S(1)} %get-tuple-element.16), channel_id=1, source_target_pairs={{1,0},{2,1},{3,2},{4,3},{5,4},{6,5},{7,6},{9,8},{10,9},{11,10},{12... | collective-permute-start | bytes 1572872 | tf_op jit(solution)/shard_map/ppermute | solution.py:21
  244.8 15.4 %copy-start.3 = (f32[8,4,128,128]{3,0,2,1:T(8,128)S(1)}, f32[8,4,128,128]{3,0,2,1:T(8,128)}, u32[]{:S(2)}) copy-start(f32[8,4,128,128]{3,0,2,1:T(8,128)} %get-tuple-element.6) | copy-start | bytes 6291460
  244.8 15.4 %copy-start.5 = (f32[8,4,128,128]{3,0,2,1:T(8,128)S(1)}, f32[8,4,128,128]{3,0,2,1:T(8,128)}, u32[]{:S(2)}) copy-start(f32[8,4,128,128]{3,0,2,1:T(8,128)} %get-tuple-element.7) | copy-start | bytes 6291460
  244.8 10.8 %collective-permute-start.7 = (f32[8,1,128,128]{3,0,2,1:T(8,128)S(1)}, f32[8,1,128,128]{3,0,2,1:T(8,128)S(1)}, u32[]{:S(2)}, u32[]{:S(2)}) collective-permute-start(f32[8,1,128,128]{3,0,2,1:T(8,128)S(1)} %get-tuple-element.15), channel_id=1, source_target_pairs={{0,1},{1,2},{2,3},{3,4},{4,5},{5,6},{6,7},{8,9},{9,10},{10,11},{11... | collective-permute-start | bytes 1572872 | tf_op jit(solution)/shard_map/ppermute | solution.py:19
  260.2 60.6 %copy-start.10 = (f32[1,8,4,128,128]{4,3,2,1,0:T(8,128)S(1)}, f32[1,8,4,128,128]{4,3,2,1,0:T(8,128)}, u32[]{:S(2)}) copy-start(f32[1,8,4,128,128]{4,3,2,1,0:T(8,128)} %param.4) | copy-start | bytes 6291460
  271.0 49.8 %collective-permute-start.9 = (f32[8,4,128,128]{3,0,2,1:T(8,128)}, f32[8,4,128,128]{3,0,2,1:T(8,128)S(1)}, u32[]{:S(2)}, u32[]{:S(2)}) collective-permute-start(f32[8,4,128,128]{3,0,2,1:T(8,128)} %bitcast_add_fusion.2), channel_id=1, source_target_pairs={{0,8},{8,16},{16,24},{1,9},{9,17},{17,25},{2,10},{10,18},{18,26},{... | collective-permute-start | bytes 6291464 | tf_op jit(solution)/shard_map/ppermute | solution.py:31
  322.2 8.6 %collective-permute-start.11 = (f32[8,1,128,128]{3,0,2,1:T(8,128)S(1)}, f32[8,1,128,128]{3,0,2,1:T(8,128)S(1)}, u32[]{:S(2)}, u32[]{:S(2)}) collective-permute-start(f32[8,1,128,128]{3,0,2,1:T(8,128)S(1)} %get-tuple-element.14), channel_id=1, source_target_pairs={{1,0},{2,1},{3,2},{4,3},{5,4},{6,5},{7,6},{9,8},{10,9},{11,10},{12... | collective-permute-start | bytes 1572872 | tf_op jit(solution)/shard_map/ppermute | solution.py:21
  324.1 10.5 %collective-permute-start.10 = (f32[8,1,128,128]{3,0,2,1:T(8,128)S(1)}, f32[8,1,128,128]{3,0,2,1:T(8,128)S(1)}, u32[]{:S(2)}, u32[]{:S(2)}) collective-permute-start(f32[8,1,128,128]{3,0,2,1:T(8,128)S(1)} %get-tuple-element.13), channel_id=1, source_target_pairs={{0,1},{1,2},{2,3},{3,4},{4,5},{5,6},{6,7},{8,9},{9,10},{10,11},{11... | collective-permute-start | bytes 1572872 | tf_op jit(solution)/shard_map/ppermute | solution.py:19
  349.8 49.7 %collective-permute-start.12 = (f32[8,4,128,128]{3,0,2,1:T(8,128)}, f32[8,4,128,128]{3,0,2,1:T(8,128)S(1)}, u32[]{:S(2)}, u32[]{:S(2)}) collective-permute-start(f32[8,4,128,128]{3,0,2,1:T(8,128)} %bitcast_add_fusion.1), channel_id=1, source_target_pairs={{0,8},{8,16},{16,24},{1,9},{9,17},{17,25},{2,10},{10,18},{18,26},{... | collective-permute-start | bytes 6291464 | tf_op jit(solution)/shard_map/ppermute | solution.py:31
  400.9 8.6 %collective-permute-start.14 = (f32[8,1,128,128]{3,0,2,1:T(8,128)S(1)}, f32[8,1,128,128]{3,0,2,1:T(8,128)S(1)}, u32[]{:S(2)}, u32[]{:S(2)}) collective-permute-start(f32[8,1,128,128]{3,0,2,1:T(8,128)S(1)} %get-tuple-element.12), channel_id=1, source_target_pairs={{1,0},{2,1},{3,2},{4,3},{5,4},{6,5},{7,6},{9,8},{10,9},{11,10},{12... | collective-permute-start | bytes 1572872 | tf_op jit(solution)/shard_map/ppermute | solution.py:21
  402.9 10.5 %collective-permute-start.13 = (f32[8,1,128,128]{3,0,2,1:T(8,128)S(1)}, f32[8,1,128,128]{3,0,2,1:T(8,128)S(1)}, u32[]{:S(2)}, u32[]{:S(2)}) collective-permute-start(f32[8,1,128,128]{3,0,2,1:T(8,128)S(1)} %get-tuple-element.11), channel_id=1, source_target_pairs={{0,1},{1,2},{2,3},{3,4},{4,5},{5,6},{6,7},{8,9},{9,10},{10,11},{11... | collective-permute-start | bytes 1572872 | tf_op jit(solution)/shard_map/ppermute | solution.py:19
  (12 other events, 100.1 us)
where the time goes:
time: 436 us; the launch traced here: 430 us
  waiting for transfers between devices  167 us (38%)
  other arithmetic  158 us (36%)
  matrix products  59.1 us (14%)
  starting transfers between devices  36.8 us (8%)
  local copies, waits for them, and re-layouts  7.87 us (2%)
    ppermute x3, waiting for transfers between devices, from_behind(): return lax.ppermute(value, axis, pairs)  143 us
    add x1, other arithmetic, body(): current_end = coarse_old + correction  61.9 us
    dot_general x1, other arithmetic, species_mix(): jnp.einsum('st,txyz->sxyz', mixing, moved, precision=lax.Precision.HIGHEST)  61 us
    dot_general x6, matrix products, species_mix(): jnp.einsum('st,txyz->sxyz', mixing, moved, precision=lax.Precision.HIGHEST)  53.6 us
    concatenate x6, other arithmetic, with_halo(): jnp.concatenate([lax.ppermute(tail, axis, [(i, (i + 1) % count) for i in...  22.2 us
    ppermute x6, starting transfers between devices, with_halo(): lax.ppermute(head, axis, [((i + 1) % count, i) for i in range(ends)])  15.6 us
    ppermute x6, starting transfers between devices, with_halo(): lax.ppermute(tail, axis, [(i, (i + 1) % count) for i in range(ends)])  13.4 us
    ppermute x6, waiting for transfers between devices, with_halo(): lax.ppermute(head, axis, [((i + 1) % count, i) for i in range(ends)])  12.8 us
  transfers between devices with their start and end apart: 15, of which 9 were waited for; matrix products, arithmetic and copies ran while one was open for 6% of the time, Pallas kernels for 0%

commit v1 on v0

v1 whole, which is shorter than its diff:
```python
import functools

import jax
import jax.numpy as jnp
from jax import lax
from jax.experimental import pallas as pl
from jax.experimental.pallas import tpu as pltpu
from jax.sharding import PartitionSpec as P

ROWS = 8
PAD = 8
fine_courant = (0.15, 0.1, 0.05)
coarse_courant = (0.3, 0.2, 0.1)


def kernel(
    TM, SP, table, mixing, starts, classes, out,
    u0, u1, w, kq, ef, ec, cl, moved,
    local_sem, cls_send, cls_recv, h0_send, h0_recv, h1_send, h1_recv,
    wh_send, wh_recv, w_send, w_recv,
):
    S, X, Y, Z = out.shape
    C = table.shape[0]
    NC = Y // ROWS
    NG = h0_send.shape[1]
    group_rows = Y // NG
    per_group = group_rows // ROWS
    tm = lax.axis_index("tm")
    sp = lax.axis_index("space")
    has_up = sp < SP - 1
    has_down = sp > 0
    has_next = tm < TM - 1
    has_prev = tm > 0

    def rows(c):
        return pl.ds(pl.multiple_of(c * ROWS, ROWS), ROWS)

    def padded_rows(c):
        return pl.ds(pl.multiple_of(c * ROWS + PAD, ROWS), ROWS)

    def remote(src, dst, send, recv, **device):
        return pltpu.make_async_remote_copy(
            src_ref=src, dst_ref=dst, send_sem=send, recv_sem=recv,
            device_id=device, device_id_type=pl.DeviceIdType.MESH,
        )

    def cls_copy(k):
        edge = X - 1 if k == 0 else 0
        place = 0 if k == 0 else X + 1
        to = sp + 1 if k == 0 else sp - 1
        return remote(classes.at[edge], cl.at[place], cls_send.at[k], cls_recv.at[k], space=to)

    def h0_copy(k, g):
        edge = X - 1 if k == 0 else 0
        place = 0 if k == 0 else X + 1
        to = sp + 1 if k == 0 else sp - 1
        src = starts.at[0, :, edge, pl.ds(pl.multiple_of(g * group_rows, ROWS), group_rows), :]
        dst = u0.at[:, place, pl.ds(pl.multiple_of(g * group_rows + PAD, ROWS), group_rows), :]
        return remote(src, dst, h0_send.at[k, g], h0_recv.at[k, g], space=to)

    def halo_copy(field, send, recv, k, c):
        edge = X if k == 0 else 1
        place = 0 if k == 0 else X + 1
        to = sp + 1 if k == 0 else sp - 1
        return remote(
            field.at[:, edge, padded_rows(c), :], field.at[:, place, padded_rows(c), :],
            send.at[k, c], recv.at[k, c], space=to,
        )

    h1_copy = functools.partial(halo_copy, u1, h1_send, h1_recv)
    wh_copy = functools.partial(halo_copy, w, wh_send, wh_recv)

    def w_copy(c):
        return remote(
            out.at[:, :, rows(c), :], w.at[:, pl.ds(1, X), padded_rows(c), :],
            w_send.at[c], w_recv.at[c], tm=tm + 1,
        )

    def start_both(copy, *args):
        pl.when(has_up)(lambda: copy(0, *args).start())
        pl.when(has_down)(lambda: copy(1, *args).start())

    def recv_both(copy, *args):
        pl.when(has_down)(lambda: copy(0, *args).wait_recv())
        pl.when(has_up)(lambda: copy(1, *args).wait_recv())

    def sent_both(copy, *args):
        pl.when(has_up)(lambda: copy(0, *args).wait_send())
        pl.when(has_down)(lambda: copy(1, *args).wait_send())

    start_in = pltpu.make_async_copy(
        starts.at[0], u0.at[:, pl.ds(1, X), pl.ds(PAD, Y), :], local_sem.at[0]
    )
    class_in = pltpu.make_async_copy(classes, cl.at[pl.ds(1, X)], local_sem.at[1])
    start_in.start()
    class_in.start()

    barrier = pltpu.get_barrier_semaphore()
    for exists, device in (
        (has_up, dict(space=sp + 1)), (has_down, dict(space=sp - 1)),
        (has_next, dict(tm=tm + 1)), (has_prev, dict(tm=tm - 1)),
    ):
        def greet(device=device):
            pl.semaphore_signal(
                barrier, inc=1, device_id=device, device_id_type=pl.DeviceIdType.MESH
            )
        pl.when(exists)(greet)

    tile_all = jnp.zeros((X + 2, PAD, Z), jnp.float32)

    def clear(s, carry):
        for field in (u0, u1, w):
            field[s, :, 0:PAD, :] = tile_all
            field[s, :, Y + PAD : Y + 2 * PAD, :] = tile_all
        outside = jnp.full((X + 2, PAD, Z), table[0, s] * 0.125, jnp.float32)
        kq[s, :, 0:PAD, :] = outside
        kq[s, :, Y + PAD : Y + 2 * PAD, :] = outside
        return carry

    lax.fori_loop(0, S, clear, 0)

    def clear_plane(place):
        def one(s, carry):
            for field in (u0, u1, w):
                field[s, place, PAD : Y + PAD, :] = jnp.zeros((Y, Z), jnp.float32)
            return carry
        lax.fori_loop(0, S, one, 0)
        cl[place] = jnp.zeros((Y, Z), jnp.int32)

    pl.when(jnp.logical_not(has_down))(lambda: clear_plane(0))
    pl.when(jnp.logical_not(has_up))(lambda: clear_plane(X + 1))

    neighbours = (
        has_up.astype(jnp.int32) + has_down.astype(jnp.int32)
        + has_next.astype(jnp.int32) + has_prev.astype(jnp.int32)
    )
    pl.semaphore_wait(barrier, neighbours)

    start_both(cls_copy)
    for g in range(NG):
        start_both(h0_copy, g)
    start_in.wait()
    class_in.wait()
    recv_both(cls_copy)

    lane = lax.broadcasted_iota(jnp.int32, (X, ROWS, Z), 2)
    at_first = lane == 0
    at_last = lane == Z - 1

    def behind(value, fill=0.0):
        return jnp.where(at_first, fill, pltpu.roll(value, 1, 2))

    def ahead(value, fill=0.0):
        return jnp.where(at_last, fill, pltpu.roll(value, Z - 1, 2))

    def three(field, s, c, inner):
        base = c * ROWS + PAD
        planes = pl.ds(1, X) if inner else slice(None)
        before = field[s, planes, pl.ds(base - 1, ROWS), :]
        here = field[s, :, padded_rows(c), :]
        after = field[s, planes, pl.ds(base + 1, ROWS), :]
        return before, here, after

    def smooth_x(value):
        middle = value[1:-1]
        return (value[:-2] + value[2:]) + (middle + middle)

    def kappa(c):
        found = cl[:, rows(c), :]
        bits = []
        level = 1
        while level < C:
            bits.append((found & level) != 0)
            level *= 2

        def one(s, carry):
            values = [table[i, s] for i in range(C)]
            for bit in bits:
                values = [
                    jnp.where(bit, values[i + 1], values[i]) if i + 1 < len(values) else values[i]
                    for i in range(0, len(values), 2)
                ]
            kq[s, :, padded_rows(c), :] = jnp.broadcast_to(values[0], found.shape) * 0.125
            return carry

        lax.fori_loop(0, S, one, 0)

    def coefficients(c):
        def one(s, carry):
            before, here, after = three(kq, s, c, False)
            outside = table[0, s] * 0.125
            mid = here[1:-1]
            smooth = smooth_x((before + after) + (here + here))
            smooth = (smooth + smooth) + (
                behind(smooth, outside * 16.0) + ahead(smooth, outside * 16.0)
            )
            ef[s, :, rows(c), :] = (1.0 - sum(fine_courant)) - 64.0 * mid - smooth
            faces = (here[:-2] + here[2:]) + (before[1:-1] + after[1:-1])
            faces = faces + (behind(mid, outside) + ahead(mid, outside))
            ec[s, :, rows(c), :] = (1.0 - sum(coarse_courant)) - 96.0 * mid - 16.0 * faces
            return carry

        lax.fori_loop(0, S, one, 0)

    def fine_move(field, s, c):
        before, here, after = three(field, s, c, False)
        k_before, k_here, k_after = three(kq, s, c, False)
        product = k_here * here
        weighted = (k_before * before + k_after * after) + (product + product)
        plain = smooth_x((before + after) + (here + here))
        weighted = smooth_x(weighted)
        mid = here[1:-1]
        result = mid * ef[s, :, rows(c), :]
        result += fine_courant[0] * here[:-2] + fine_courant[1] * before[1:-1]
        result += k_here[1:-1] * ((plain + plain) + (behind(plain) + ahead(plain)))
        result += (weighted + weighted) + (
            behind(weighted + fine_courant[2] * mid) + ahead(weighted)
        )
        return result

    def coarse_move(field, s, c):
        before, here, after = three(field, s, c, True)
        k_before, k_here, k_after = three(kq, s, c, True)
        mid = here[1:-1]
        k_mid = k_here[1:-1]
        product = k_here * here
        mid_product = product[1:-1]
        plain = (here[:-2] + here[2:]) + (before + after)
        plain = plain + (behind(mid) + ahead(mid))
        weighted = (product[:-2] + product[2:]) + (k_before * before + k_after * after)
        weighted = weighted + (
            behind(mid_product + (coarse_courant[2] / 16.0) * mid) + ahead(mid_product)
        )
        result = mid * ec[s, :, rows(c), :]
        result += coarse_courant[0] * here[:-2] + coarse_courant[1] * before
        return result + 16.0 * (k_mid * plain + weighted)

    def mix(store):
        values = [moved[t] for t in range(S)]
        for s in range(S):
            total = mixing[s, 0] * values[0]
            for t in range(1, S):
                total += mixing[s, t] * values[t]
            store(s, total)

    def each_species(move):
        def one(s, carry):
            moved[s] = move(s)
            return carry
        lax.fori_loop(0, S, one, 0)

    def first_fine(c):
        each_species(lambda s: fine_move(u0, s, c))

        def store(s, value):
            u1[s, 1 : X + 1, padded_rows(c), :] = value

        mix(store)
        start_both(h1_copy, c)

    def store_out(c):
        def store(s, value):
            out[s, :, rows(c), :] = value
        return store

    def second_fine(c):
        @pl.when(jnp.logical_not(has_prev))
        def _():
            each_species(lambda s: fine_move(u1, s, c))
            mix(store_out(c))
            pl.when(has_next)(lambda: w_copy(c).start())

        @pl.when(has_prev)
        def _():
            each_species(lambda s: fine_move(u1, s, c) - coarse_move(u0, s, c))
            mix(store_out(c))

    def own_step(t, carry):
        @pl.when(t < NC)
        def _():
            pl.when(lax.rem(t, per_group) == 0)(lambda: recv_both(h0_copy, t // per_group))
            kappa(t)

        @pl.when(jnp.logical_and(t >= 1, t <= NC))
        def _():
            coefficients(t - 1)
            first_fine(t - 1)

        @pl.when(jnp.logical_and(t >= 2, t <= NC + 1))
        def _():
            recv_both(h1_copy, t - 2)

        pl.when(t >= 3)(lambda: second_fine(t - 3))
        return carry

    lax.fori_loop(0, NC + 3, own_step, 0)

    def chain_step(t, carry):
        @pl.when(t < NC)
        def _():
            w_copy(t).wait_recv()
            start_both(wh_copy, t)

        @pl.when(t >= 1)
        def _():
            c = t - 1
            recv_both(wh_copy, c)
            each_species(lambda s: coarse_move(w, s, c))

            def store(s, value):
                out[s, :, rows(c), :] = out[s, :, rows(c), :] + value

            mix(store)
            pl.when(has_next)(lambda: w_copy(c).start())
        return carry

    @pl.when(has_prev)
    def _():
        lax.fori_loop(0, NC + 1, chain_step, 0)

    sent_both(cls_copy)
    for g in range(NG):
        sent_both(h0_copy, g)

    def finish(c, carry):
        sent_both(h1_copy, c)
        pl.when(has_prev)(lambda: sent_both(wh_copy, c))
        pl.when(has_next)(lambda: w_copy(c).wait_send())
        return carry

    lax.fori_loop(0, NC, finish, 0)


def solution(mesh):
    TM, SP = mesh.shape["tm"], mesh.shape["space"]

    def body(starts, classes, table, mixing):
        _, S, X, Y, Z = starts.shape
        NC = Y // ROWS
        NG = 4
        padded = pltpu.VMEM((S, X + 2, Y + 2 * PAD, Z), jnp.float32)
        plain = pltpu.VMEM((S, X, Y, Z), jnp.float32)
        dma = pltpu.SemaphoreType.DMA
        result = pl.pallas_call(
            functools.partial(kernel, TM, SP),
            out_shape=jax.ShapeDtypeStruct((S, X, Y, Z), jnp.float32),
            in_specs=[
                pl.BlockSpec(memory_space=pltpu.SMEM),
                pl.BlockSpec(memory_space=pltpu.SMEM),
                pl.BlockSpec(memory_space=pl.ANY),
                pl.BlockSpec(memory_space=pl.ANY),
            ],
            out_specs=pl.BlockSpec(memory_space=pltpu.VMEM),
            scratch_shapes=[
                padded, padded, padded, padded, plain, plain,
                pltpu.VMEM((X + 2, Y, Z), jnp.int32),
                pltpu.VMEM((S, X, ROWS, Z), jnp.float32),
                dma((2,)), dma((2,)), dma((2,)), dma((2, NG)), dma((2, NG)),
                dma((2, NC)), dma((2, NC)), dma((2, NC)), dma((2, NC)),
                dma((NC,)), dma((NC,)),
            ],
            compiler_params=pltpu.CompilerParams(
                collective_id=0, has_side_effects=True, vmem_limit_bytes=48 * 1024 * 1024
            ),
        )(table, mixing, starts, classes)
        return result[None]

    in_specs = (P("tm", None, "space", None, None), P("space", None, None), P(), P())
    out_specs = P("tm", None, "space", None, None)
    return jax.shard_map(body, mesh=mesh, in_specs=in_specs, out_specs=out_specs, check_vma=False)
```

time: 436 us -> 125 us (0.29)
  the two profiles are of different devices: /device:TPU:12 before, /device:TPU:15 now
where the time goes in v1:
time: 125 us; the launch traced here: 124 us
  Pallas kernels  119 us (95%)
  local copies, waits for them, and re-layouts  5.3 us (4%)
    pallas_call x1, Pallas kernels, body(): pl.pallas_call(functools.partial(kernel, TM, SP), out_shape=jax.ShapeDtyp...  119 us
    unnamed x8, local copies, waits for them, and re-layouts  5.3 us

profile of v1, /device:TPU:15, one launch (start us, length us, event | category | flops | bytes accessed | tf_op | source)
XLA Modules:
  0.0 124.3 jit_solution(10416418476953133977)
XLA Ops:
  0.0 0.8 copy.5.table
  0.8 0.0 copy-start
  0.8 1.6 %copy-done = f32[1,8,4,128,128]{4,3,2,1,0:T(8,128)S(1)} copy-done((f32[1,8,4,128,128]{4,3,2,1,0:T(8,128)S(1)}, f32[1,8,4,128,128]{4,3,2,1,0:T(8,128)}, u32[]{:S(2)}) %copy-start) | copy-done | bytes 2097176
  2.3 0.0 copy-start.1
  2.4 0.9 copy-done.1
  3.3 0.0 copy-start.2
  3.3 0.7 copy-done.2
  4.0 119.0 %shard_map.46 = f32[8,4,128,128]{3,2,1,0:T(8,128)S(1)} custom-call(f32[16,8]{1,0:T(8,128)S(1)} %copy.5.table, f32[8,8]{1,0:T(8,128)S(1)} %copy-done.2, f32[1,8,4,128,128]{4,3,2,1,0:T(8,128)S(1)} %copy-done, s32[4,128,128]{2,1,0:T(8,128)S(1)} %copy-done.1), custom_call_target="tpu_custom_call" | custom-call | tf_op jit(solution)/shard_map/pallas_call | solution.py:344
  123.0 1.3 %copy.7 = f32[1,8,4,128,128]{4,3,2,1,0:T(8,128)} copy(f32[1,8,4,128,128]{4,3,2,1,0:T(8,128)S(1)} %bitcast.1) | data formatting | bytes 4194304
Async XLA Ops:
  0.8 1.6 %copy-start = (f32[1,8,4,128,128]{4,3,2,1,0:T(8,128)S(1)}, f32[1,8,4,128,128]{4,3,2,1,0:T(8,128)}, u32[]{:S(2)}) copy-start(f32[1,8,4,128,128]{4,3,2,1,0:T(8,128)} %starts.1) | copy-start | bytes 6291460
  2.3 0.9 copy-start.1
  3.3 0.7 copy-start.2

commit v2 on v1

--- a/solution.py
+++ b/solution.py
@@ -8,6 +8,10 @@
 from jax.sharding import PartitionSpec as P
 
 ROWS = 8
+BEHIND = 4
+LAG = 2
+LAG0 = 0
+UNROLL = 4
 PAD = 8
 fine_courant = (0.15, 0.1, 0.05)
 coarse_courant = (0.3, 0.2, 0.1)
@@ -20,7 +24,7 @@
     wh_send, wh_recv, w_send, w_recv,
 ):
     S, X, Y, Z = out.shape
-    C = table.shape[0]
+    C = table.shape[1]
     NC = Y // ROWS
     NG = h0_send.shape[1]
     group_rows = Y // NG
@@ -112,7 +116,7 @@
         for field in (u0, u1, w):
             field[s, :, 0:PAD, :] = tile_all
             field[s, :, Y + PAD : Y + 2 * PAD, :] = tile_all
-        outside = jnp.full((X + 2, PAD, Z), table[0, s] * 0.125, jnp.float32)
+        outside = jnp.full((X + 2, PAD, Z), table[s, 0] * 0.125, jnp.float32)
         kq[s, :, 0:PAD, :] = outside
         kq[s, :, Y + PAD : Y + 2 * PAD, :] = outside
         return carry
@@ -124,7 +128,7 @@
             for field in (u0, u1, w):
                 field[s, place, PAD : Y + PAD, :] = jnp.zeros((Y, Z), jnp.float32)
             return carry
-        lax.fori_loop(0, S, one, 0)
+        lax.fori_loop(0, S, one, 0, unroll=UNROLL)
         cl[place] = jnp.zeros((Y, Z), jnp.int32)
 
     pl.when(jnp.logical_not(has_down))(lambda: clear_plane(0))
@@ -174,7 +178,7 @@
             level *= 2
 
         def one(s, carry):
-            values = [table[i, s] for i in range(C)]
+            values = [table[s, i] for i in range(C)]
             for bit in bits:
                 values = [
                     jnp.where(bit, values[i + 1], values[i]) if i + 1 < len(values) else values[i]
@@ -183,12 +187,12 @@
             kq[s, :, padded_rows(c), :] = jnp.broadcast_to(values[0], found.shape) * 0.125
             return carry
 
-        lax.fori_loop(0, S, one, 0)
+        lax.fori_loop(0, S, one, 0, unroll=UNROLL)
 
     def coefficients(c):
         def one(s, carry):
             before, here, after = three(kq, s, c, False)
-            outside = table[0, s] * 0.125
+            outside = table[s, 0] * 0.125
             mid = here[1:-1]
             smooth = smooth_x((before + after) + (here + here))
             smooth = (smooth + smooth) + (
@@ -200,7 +204,7 @@
             ec[s, :, rows(c), :] = (1.0 - sum(coarse_courant)) - 96.0 * mid - 16.0 * faces
             return carry
 
-        lax.fori_loop(0, S, one, 0)
+        lax.fori_loop(0, S, one, 0, unroll=UNROLL)
 
     def fine_move(field, s, c):
         before, here, after = three(field, s, c, False)
@@ -247,7 +251,7 @@
         def one(s, carry):
             moved[s] = move(s)
             return carry
-        lax.fori_loop(0, S, one, 0)
+        lax.fori_loop(0, S, one, 0, unroll=UNROLL)
 
     def first_fine(c):
         each_species(lambda s: fine_move(u0, s, c))
@@ -275,7 +279,7 @@
             each_species(lambda s: fine_move(u1, s, c) - coarse_move(u0, s, c))
             mix(store_out(c))
 
-    def own_step(t, carry):
+    def own_step(t):
         @pl.when(t < NC)
         def _():
             pl.when(lax.rem(t, per_group) == 0)(lambda: recv_both(h0_copy, t // per_group))
@@ -286,16 +290,13 @@
             coefficients(t - 1)
             first_fine(t - 1)
 
-        @pl.when(jnp.logical_and(t >= 2, t <= NC + 1))
-        def _():
-            recv_both(h1_copy, t - 2)
-
-        pl.when(t >= 3)(lambda: second_fine(t - 3))
-        return carry
-
-    lax.fori_loop(0, NC + 3, own_step, 0)
-
-    def chain_step(t, carry):
+        @pl.when(jnp.logical_and(t >= BEHIND - 1, t <= NC + BEHIND - 2))
+        def _():
+            recv_both(h1_copy, t - (BEHIND - 1))
+
+        pl.when(jnp.logical_and(t >= BEHIND, t < NC + BEHIND))(lambda: second_fine(t - BEHIND))
+
+    def chain_step(t):
         @pl.when(t < NC)
         def _():
             w_copy(t).wait_recv()
@@ -312,11 +313,19 @@
 
             mix(store)
             pl.when(has_next)(lambda: w_copy(c).start())
+
+    chain_from = BEHIND + LAG * tm + LAG0
+
+    def step(t, carry):
+        chain_t = t - chain_from
+        pl.when(jnp.logical_and(has_prev, jnp.logical_and(chain_t >= 0, chain_t <= NC)))(
+            lambda: chain_step(chain_t)
+        )
+        pl.when(t < NC + BEHIND)(lambda: own_step(t))
         return carry
 
-    @pl.when(has_prev)
-    def _():
-        lax.fori_loop(0, NC + 1, chain_step, 0)
+    steps = jnp.where(has_prev, chain_from + NC + 1, NC + BEHIND)
+    lax.fori_loop(0, steps, step, 0)
 
     sent_both(cls_copy)
     for g in range(NG):
@@ -362,7 +371,7 @@
             compiler_params=pltpu.CompilerParams(
                 collective_id=0, has_side_effects=True, vmem_limit_bytes=48 * 1024 * 1024
             ),
-        )(table, mixing, starts, classes)
+        )(table.T, mixing, starts, classes)
         return result[None]
 
     in_specs = (P("tm", None, "space", None, None), P("space", None, None), P(), P())

time: 125 us -> 86.7 us (0.69)
  Pallas kernels: 119 us -> 81.2 us
    pallas_call x1, Pallas kernels: 119 us -> 81.2 us  [body(): pl.pallas_call(functools.partial(kernel, TM, SP), out_shape=jax.ShapeDtyp...]
    unnamed x8 -> x9, local copies, waits for them, and re-layouts: 5.3 us -> 5.23 us
where the time goes in v2:
time: 86.7 us; the launch traced here: 86.4 us
  Pallas kernels  81.2 us (94%)
  local copies, waits for them, and re-layouts  5.23 us (6%)
    pallas_call x1, Pallas kernels, body(): pl.pallas_call(functools.partial(kernel, TM, SP), out_shape=jax.ShapeDtyp...  81.2 us
    unnamed x9, local copies, waits for them, and re-layouts  5.23 us

profile of v2, /device:TPU:15, one launch (start us, length us, event | category | flops | bytes accessed | tf_op | source)
XLA Modules:
  0.0 86.4 jit_solution(1212387085761217563)
XLA Ops:
  0.0 0.0 copy-start
  0.0 1.6 %copy-done = f32[1,8,4,128,128]{4,3,2,1,0:T(8,128)S(1)} copy-done((f32[1,8,4,128,128]{4,3,2,1,0:T(8,128)S(1)}, f32[1,8,4,128,128]{4,3,2,1,0:T(8,128)}, u32[]{:S(2)}) %copy-start) | copy-done | bytes 2097176
  1.6 0.0 copy-start.1
  1.6 0.9 %copy-done.1 = s32[4,128,128]{2,1,0:T(8,128)S(1)} copy-done((s32[4,128,128]{2,1,0:T(8,128)S(1)}, s32[4,128,128]{2,1,0:T(8,128)}, u32[]{:S(2)}) %copy-start.1) | copy-done | bytes 262168
  2.5 0.0 copy-start.2
  2.5 0.7 copy-done.2
  3.2 0.0 copy-start.3
  3.2 0.7 copy-done.3
  3.9 81.2 %shard_map.46 = f32[8,4,128,128]{3,2,1,0:T(8,128)S(1)} custom-call(f32[8,16]{1,0:T(8,128)S(1)} %bitcast.3, f32[8,8]{1,0:T(8,128)S(1)} %copy-done.3, f32[1,8,4,128,128]{4,3,2,1,0:T(8,128)S(1)} %copy-done, s32[4,128,128]{2,1,0:T(8,128)S(1)} %copy-done.1), custom_call_target="tpu_custom_call" | custom-call | tf_op jit(solution)/shard_map/pallas_call | solution.py:353
  85.1 1.3 %copy.6 = f32[1,8,4,128,128]{4,3,2,1,0:T(8,128)} copy(f32[1,8,4,128,128]{4,3,2,1,0:T(8,128)S(1)} %bitcast.2) | data formatting | bytes 4194304
Async XLA Ops:
  0.0 1.6 %copy-start = (f32[1,8,4,128,128]{4,3,2,1,0:T(8,128)S(1)}, f32[1,8,4,128,128]{4,3,2,1,0:T(8,128)}, u32[]{:S(2)}) copy-start(f32[1,8,4,128,128]{4,3,2,1,0:T(8,128)} %starts.1) | copy-start | bytes 6291460
  1.6 0.9 %copy-start.1 = (s32[4,128,128]{2,1,0:T(8,128)S(1)}, s32[4,128,128]{2,1,0:T(8,128)}, u32[]{:S(2)}) copy-start(s32[4,128,128]{2,1,0:T(8,128)} %classes.1) | copy-start | bytes 786436
  2.5 0.7 copy-start.2
  3.2 0.7 copy-start.3

commit v3 on v2

--- a/solution.py
+++ b/solution.py
@@ -11,15 +11,15 @@
 BEHIND = 4
 LAG = 2
 LAG0 = 0
-UNROLL = 4
+UNROLL = 8
 PAD = 8
 fine_courant = (0.15, 0.1, 0.05)
 coarse_courant = (0.3, 0.2, 0.1)
 
 
 def kernel(
-    TM, SP, table, mixing, starts, classes, out,
-    u0, u1, w, kq, ef, ec, cl, moved,
+    TM, SP, table_in, mixing_in, starts, classes, out,
+    table, mixing, u0, u1, w, kq, ef, ec, cl, moved,
     local_sem, cls_send, cls_recv, h0_send, h0_recv, h1_send, h1_recv,
     wh_send, wh_recv, w_send, w_recv,
 ):
@@ -96,8 +96,12 @@
         starts.at[0], u0.at[:, pl.ds(1, X), pl.ds(PAD, Y), :], local_sem.at[0]
     )
     class_in = pltpu.make_async_copy(classes, cl.at[pl.ds(1, X)], local_sem.at[1])
+    table_copy = pltpu.make_async_copy(table_in, table, local_sem.at[2])
+    mixing_copy = pltpu.make_async_copy(mixing_in, mixing, local_sem.at[3])
+    table_copy.start()
+    class_in.start()
     start_in.start()
-    class_in.start()
+    mixing_copy.start()
 
     barrier = pltpu.get_barrier_semaphore()
     for exists, device in (
@@ -116,12 +120,16 @@
         for field in (u0, u1, w):
             field[s, :, 0:PAD, :] = tile_all
             field[s, :, Y + PAD : Y + 2 * PAD, :] = tile_all
+        return carry
+
+    def outside_rows(s, carry):
         outside = jnp.full((X + 2, PAD, Z), table[s, 0] * 0.125, jnp.float32)
         kq[s, :, 0:PAD, :] = outside
         kq[s, :, Y + PAD : Y + 2 * PAD, :] = outside
         return carry
 
     lax.fori_loop(0, S, clear, 0)
+
 
     def clear_plane(place):
         def one(s, carry):
@@ -143,6 +151,9 @@
     start_both(cls_copy)
     for g in range(NG):
         start_both(h0_copy, g)
+    table_copy.wait()
+    lax.fori_loop(0, S, outside_rows, 0)
+    mixing_copy.wait()
     start_in.wait()
     class_in.wait()
     recv_both(cls_copy)
@@ -189,7 +200,7 @@
 
         lax.fori_loop(0, S, one, 0, unroll=UNROLL)
 
-    def coefficients(c):
+    def coefficients(c, with_coarse):
         def one(s, carry):
             before, here, after = three(kq, s, c, False)
             outside = table[s, 0] * 0.125
@@ -199,6 +210,8 @@
                 behind(smooth, outside * 16.0) + ahead(smooth, outside * 16.0)
             )
             ef[s, :, rows(c), :] = (1.0 - sum(fine_courant)) - 64.0 * mid - smooth
+            if not with_coarse:
+                return carry
             faces = (here[:-2] + here[2:]) + (before[1:-1] + after[1:-1])
             faces = faces + (behind(mid, outside) + ahead(mid, outside))
             ec[s, :, rows(c), :] = (1.0 - sum(coarse_courant)) - 96.0 * mid - 16.0 * faces
@@ -287,7 +300,8 @@
 
         @pl.when(jnp.logical_and(t >= 1, t <= NC))
         def _():
-            coefficients(t - 1)
+            pl.when(has_prev)(lambda: coefficients(t - 1, True))
+            pl.when(jnp.logical_not(has_prev))(lambda: coefficients(t - 1, False))
             first_fine(t - 1)
 
         @pl.when(jnp.logical_and(t >= BEHIND - 1, t <= NC + BEHIND - 2))
@@ -354,22 +368,24 @@
             functools.partial(kernel, TM, SP),
             out_shape=jax.ShapeDtypeStruct((S, X, Y, Z), jnp.float32),
             in_specs=[
-                pl.BlockSpec(memory_space=pltpu.SMEM),
-                pl.BlockSpec(memory_space=pltpu.SMEM),
-                pl.BlockSpec(memory_space=pl.ANY),
-                pl.BlockSpec(memory_space=pl.ANY),
+                pl.BlockSpec(memory_space=pltpu.HBM),
+                pl.BlockSpec(memory_space=pltpu.HBM),
+                pl.BlockSpec(memory_space=pltpu.HBM),
+                pl.BlockSpec(memory_space=pltpu.HBM),
             ],
             out_specs=pl.BlockSpec(memory_space=pltpu.VMEM),
             scratch_shapes=[
+                pltpu.SMEM(table.shape[::-1], jnp.float32),
+                pltpu.SMEM(mixing.shape, jnp.float32),
                 padded, padded, padded, padded, plain, plain,
                 pltpu.VMEM((X + 2, Y, Z), jnp.int32),
                 pltpu.VMEM((S, X, ROWS, Z), jnp.float32),
-                dma((2,)), dma((2,)), dma((2,)), dma((2, NG)), dma((2, NG)),
+                dma((4,)), dma((2,)), dma((2,)), dma((2, NG)), dma((2, NG)),
                 dma((2, NC)), dma((2, NC)), dma((2, NC)), dma((2, NC)),
                 dma((NC,)), dma((NC,)),
             ],
             compiler_params=pltpu.CompilerParams(
-                collective_id=0, has_side_effects=True, vmem_limit_bytes=48 * 1024 * 1024
+                collective_id=0, has_side_effects=True, vmem_limit_bytes=62 * 1024 * 1024
             ),
         )(table.T, mixing, starts, classes)
         return result[None]

time: 86.7 us -> 84.5 us (0.975)
  local copies, waits for them, and re-layouts: 5.23 us -> 3.14 us
    unnamed x9 -> x1, local copies, waits for them, and re-layouts: 5.23 us -> 3.14 us
where the time goes in v3:
time: 84.5 us; the launch traced here: 84.3 us
  Pallas kernels  81.2 us (96%)
  local copies, waits for them, and re-layouts  3.14 us (4%)
    pallas_call x1, Pallas kernels, body(): pl.pallas_call(functools.partial(kernel, TM, SP), out_shape=jax.ShapeDtyp...  81.2 us
    unnamed x1, local copies, waits for them, and re-layouts  3.14 us

profile of v3, /device:TPU:15, one launch (start us, length us, event | category | flops | bytes accessed | tf_op | source)
XLA Modules:
  0.0 84.3 jit_solution(10748936752889035333)
XLA Ops:
  0.0 81.2 %shard_map.46 = f32[8,4,128,128]{3,2,1,0:T(8,128)} custom-call(f32[8,16]{1,0:T(8,128)} %bitcast.3, f32[8,8]{1,0:T(8,128)} %mixing_in.1, f32[1,8,4,128,128]{4,3,2,1,0:T(8,128)} %starts.1, s32[4,128,128]{2,1,0:T(8,128)} %classes.1), custom_call_target="tpu_custom_call" | custom-call | tf_op jit(solution)/shard_map/pallas_call | solution.py:367
  81.2 3.1 %copy.6 = f32[1,8,4,128,128]{4,3,2,1,0:T(8,128)} copy(f32[1,8,4,128,128]{4,3,2,1,0:T(8,128)} %bitcast.2) | data formatting | bytes 4194304

commit v4 on v3

--- a/solution.py
+++ b/solution.py
@@ -18,8 +18,8 @@
 
 
 def kernel(
-    TM, SP, table_in, mixing_in, starts, classes, out,
-    table, mixing, u0, u1, w, kq, ef, ec, cl, moved,
+    TM, SP, table_in, mixing_in, starts, classes, out_far,
+    out, out_sem, table, mixing, u0, u1, w, kq, ef, ec, cl, moved,
     local_sem, cls_send, cls_recv, h0_send, h0_recv, h1_send, h1_recv,
     wh_send, wh_recv, w_send, w_recv,
 ):
@@ -78,6 +78,11 @@
         return remote(
             out.at[:, :, rows(c), :], w.at[:, pl.ds(1, X), padded_rows(c), :],
             w_send.at[c], w_recv.at[c], tm=tm + 1,
+        )
+
+    def out_copy(c):
+        return pltpu.make_async_copy(
+            out.at[:, :, rows(c), :], out_far.at[:, :, rows(c), :], out_sem.at[c]
         )
 
     def start_both(copy, *args):
@@ -286,6 +291,7 @@
             each_species(lambda s: fine_move(u1, s, c))
             mix(store_out(c))
             pl.when(has_next)(lambda: w_copy(c).start())
+            out_copy(c).start()
 
         @pl.when(has_prev)
         def _():
@@ -327,6 +333,7 @@
 
             mix(store)
             pl.when(has_next)(lambda: w_copy(c).start())
+            out_copy(c).start()
 
     chain_from = BEHIND + LAG * tm + LAG0
 
@@ -349,6 +356,7 @@
         sent_both(h1_copy, c)
         pl.when(has_prev)(lambda: sent_both(wh_copy, c))
         pl.when(has_next)(lambda: w_copy(c).wait_send())
+        out_copy(c).wait()
         return carry
 
     lax.fori_loop(0, NC, finish, 0)
@@ -373,8 +381,9 @@
                 pl.BlockSpec(memory_space=pltpu.HBM),
                 pl.BlockSpec(memory_space=pltpu.HBM),
             ],
-            out_specs=pl.BlockSpec(memory_space=pltpu.VMEM),
+            out_specs=pl.BlockSpec(memory_space=pltpu.HBM),
             scratch_shapes=[
+                plain, dma((NC,)),
                 pltpu.SMEM(table.shape[::-1], jnp.float32),
                 pltpu.SMEM(mixing.shape, jnp.float32),
                 padded, padded, padded, padded, plain, plain,

time: 84.5 us -> 83.7 us (level)
  no operation moved by 1% of the time
where the time goes in v4:
time: 83.7 us; the launch traced here: 83.6 us
  Pallas kernels  80.5 us (96%)
  local copies, waits for them, and re-layouts  3.14 us (4%)
    pallas_call x1, Pallas kernels, body(): pl.pallas_call(functools.partial(kernel, TM, SP), out_shape=jax.ShapeDtyp...  80.5 us
    unnamed x1, local copies, waits for them, and re-layouts  3.14 us

profile of v4, /device:TPU:15, one launch (start us, length us, event | category | flops | bytes accessed | tf_op | source)
XLA Modules:
  0.0 83.6 jit_solution(2526158570283290180)
XLA Ops:
  0.0 80.5 %shard_map.46 = f32[8,4,128,128]{3,2,1,0:T(8,128)} custom-call(f32[8,16]{1,0:T(8,128)} %bitcast.3, f32[8,8]{1,0:T(8,128)} %mixing_in.1, f32[1,8,4,128,128]{4,3,2,1,0:T(8,128)} %starts.1, s32[4,128,128]{2,1,0:T(8,128)} %classes.1), custom_call_target="tpu_custom_call" | custom-call | tf_op jit(solution)/shard_map/pallas_call | solution.py:375
  80.5 3.1 %copy.6 = f32[1,8,4,128,128]{4,3,2,1,0:T(8,128)} copy(f32[1,8,4,128,128]{4,3,2,1,0:T(8,128)} %bitcast.2) | data formatting | bytes 4194304
